TPU v7x, 256 devices: a whole 4x4x8 slice. The times are simulated.
256 devices in a mesh: occ: 32 (over x_lo, z, core), aux: 8 (over y, x_hi).
Axes of the slice: x: 4 (x_hi: 2, x_lo: 2; x = x_hi * 2 + x_lo), y: 4, z: 8, core: 2. Of those that a mesh axis runs over, the one named last changes fastest.
Arguments:
- three_index: bfloat16 [32, 1000, 4096], P('occ', None, 'aux'), may hold values from -0.75 to 0.75
- occ_energy: float32 [32], replicated, may hold values from -2 to -0.5
- vir_energy: float32 [1000], replicated, may hold values from 0.3 to 3
Outputs:
- gamma: float32 [32, 1000, 4096], P('occ', None, 'aux')
All inputs are finite; a program needn't handle non-finite values.
Results may differ from a plain program's by a relative error of at most 0.0018.
Values may be sent and summed in bfloat16 or wider, within the bound.
A program may use at most 128 MiB of HBM per device.

v0:
```python
import jax
import jax.numpy as jnp
from jax import lax
from jax.sharding import PartitionSpec as P

STEPS = 2


def passed_along(block, axis, distance):
    devices = range(lax.axis_size(axis))
    route = [((i - distance) % len(devices), i) for i in devices]
    return lax.ppermute(block, axis, route)


def local(three_index, occ_energy, vir_energy):
    mine = three_index[0]
    n_occ = lax.axis_size("occ")
    here = lax.axis_index("occ")
    e_here = occ_energy[here]

    def amplitudes(k_part, e_other):
        k_rows = lax.psum_scatter(k_part, "aux", scatter_dimension=0, tiled=True)
        k_full = lax.all_gather(k_rows, "aux", axis=0, tiled=True)
        denom = vir_energy[:, None] + vir_energy[None, :] - e_here - e_other
        return (k_full / denom).astype(jnp.bfloat16)

    def pair_product(left, right):
        return lax.dot_general(
            left, right, (((1,), (1,)), ((), ())), preferred_element_type=jnp.float32
        )

    amp_self = amplitudes(pair_product(mine, mine), e_here)
    gamma = jnp.dot(amp_self, mine, preferred_element_type=jnp.float32)
    current = mine
    returns = []
    for step in range(1, STEPS + 1):
        current = passed_along(current, "occ", 1)
        e_other = occ_energy[(here - step) % n_occ]
        amp_pair = amplitudes(pair_product(mine, current), e_other)
        gamma = gamma + jnp.dot(amp_pair, current, preferred_element_type=jnp.float32)
        returns.append(
            lax.dot_general(
                amp_pair, mine, (((0,), (0,)), ((), ())), preferred_element_type=jnp.float32
            )
        )
    for step in range(1, STEPS + 1):
        gamma = gamma + passed_along(returns[step - 1], "occ", -step)
    return gamma[None]


def solution(mesh):
    placed = (P("occ", None, "aux"), P(), P())
    return jax.shard_map(
        local, mesh=mesh, in_specs=placed, out_specs=P("occ", None, "aux"), check_vma=False
    )
```

profile of v0, /device:TPU:2, one launch (start us, length us, event | category | flops | bytes accessed | tf_op | source)
XLA Modules:
  0.0 859.7 jit_solution(3065717121779803058)
XLA Ops:
  6.5 17.8 %collective-permute-done = bf16[1000,512]{1,0:T(8,128)(2,1)S(1)} collective-permute-done((bf16[1000,512]{1,0:T(8,128)(2,1)}, bf16[1000,512]{1,0:T(8,128)(2,1)S(1)}, u32[]{:S(2)}, u32[]{:S(2)}) %collective-permute-start) | collective-permute-done | bytes 1024032 | tf_op jit(solution)/shard_map/ppermute | solution.py:12
  24.3 5.1 fusion.10
  29.4 3.2 fusion.7
  32.6 7.8 collective-permute-done.1
  41.4 3.2 fusion.5
  46.5 491.9 %all-reduce.6.cloned.1.call-done = (f32[1000,1000]{0,1:T(8,128)}, f32[1000,1000]{0,1:T(8,128)}, f32[1000,1000]{0,1:T(8,128)}) async-done(((f32[1000,1000]{0,1:T(8,128)}, f32[1000,1000]{0,1:T(8,128)}, f32[1000,1000]{0,1:T(8,128)}), (f32[1000,1000]{0,1:T(8,128)}, f32[1000,1000]{0,1:T(8,128)}, f32[1000,1000]{0,1:T(8,128)})) %all-reduce.6.cloned.1.call-update) | async-done | bytes 12000016
  540.7 2.2 dynamic-slice_bitcast_fusion
  542.9 2.2 dynamic-slice_bitcast_fusion.2
  545.9 71.2 %all-gather.9.cloned.1.call-done = f32[8,125,1000]{1,2,0:T(8,128)} async-done(((f32[1,125,1000]{1,2,0:T(8,128)}), f32[8,125,1000]{1,2,0:T(8,128)}) %all-gather.9.cloned.1.call-update) | async-done | bytes 4000016 | tf_op jit(solution)/shard_map/all_gather | solution.py:23
  617.1 4.9 copy.8
  622.0 5.1 reshape.5
  627.1 66.2 %all-gather.11.cloned.1.call-done = f32[8,125,1000]{1,2,0:T(8,128)} async-done(((f32[1,125,1000]{1,2,0:T(8,128)}), f32[8,125,1000]{1,2,0:T(8,128)}) %all-gather.11.cloned.1.call-update) | async-done | bytes 4000016 | tf_op jit(solution)/shard_map/all_gather | solution.py:23
  693.3 4.9 copy.9
  698.2 5.2 reshape.7
  703.3 6.5 divide_convert_fusion.1
  709.9 2.5 fusion.1
  712.4 4.2 collective-permute-start.3
  716.6 2.6 fusion.3
  719.3 112.8 %all-gather.7.cloned.1.call-done = f32[8,125,1000]{1,2,0:T(8,128)} async-done(((f32[1,125,1000]{1,2,0:T(8,128)}), f32[8,125,1000]{1,2,0:T(8,128)}) %all-gather.7.cloned.1.call-update) | async-done | bytes 4000016 | tf_op jit(solution)/shard_map/all_gather | solution.py:23
  832.2 4.9 copy.7
  837.1 5.1 reshape.3
  842.2 3.2 fusion.13
  845.5 2.7 fusion
  848.1 5.0 add_bitcast_fusion
  (34 shorter events, 5.5 us)
Async XLA Ops:
  6.5 22.8 %copy-start = (bf16[1,1000,512]{2,1,0:T(8,128)(2,1)S(1)}, bf16[1,1000,512]{2,1,0:T(8,128)(2,1)}, u32[]{:S(2)}) copy-start(bf16[1,1000,512]{2,1,0:T(8,128)(2,1)} %param.3) | copy-start | bytes 3072004
  6.5 531.8 %all-reduce.6.cloned.1.call-start = ((), (), s32[]{:S(2)}) async-start(), calls=%async_computation.3 | async-start | bytes 24576000
  6.5 17.8 %collective-permute-start = (bf16[1000,512]{1,0:T(8,128)(2,1)}, bf16[1000,512]{1,0:T(8,128)(2,1)S(1)}, u32[]{:S(2)}, u32[]{:S(2)}) collective-permute-start(bf16[1000,512]{1,0:T(8,128)(2,1)} %bitcast.45), channel_id=1, source_target_pairs={{248,0},{0,8},{8,16},{16,24},{24,32},{32,40},{40,48},{48,56},{56,6... | collective-permute-start | bytes 3072008 | tf_op jit(solution)/shard_map/ppermute | solution.py:12
  24.3 8.3 copy-start.5
  24.3 16.1 %collective-permute-start.1 = (bf16[1000,512]{1,0:T(8,128)(2,1)S(1)}, bf16[1000,512]{1,0:T(8,128)(2,1)S(1)}, u32[]{:S(2)}, u32[]{:S(2)}) collective-permute-start(bf16[1000,512]{1,0:T(8,128)(2,1)S(1)} %collective-permute-done), channel_id=1, source_target_pairs={{248,0},{0,8},{8,16},{16,24},{24,32},{32,40},{40,48},{48,56},{56,6... | collective-permute-start | bytes 3072008 | tf_op jit(solution)/shard_map/ppermute | solution.py:12
  40.4 1.0 copy-start.1
  44.6 0.7 copy-start.8
  44.6 500.6 %copy-start.7 = (f32[32]{0:T(128)S(1)}, f32[32]{0:T(128)}, u32[]{:S(2)}) copy-start(f32[32]{0:T(128)} %param.4) | copy-start | bytes 388
  44.6 572.5 %all-gather.9.cloned.1.call-start = ((), (), s32[]{:S(2)}) async-start(), calls=%async_computation.1 | async-start | bytes 4608000 | tf_op jit(solution)/shard_map/all_gather | solution.py:23
  540.6 152.7 %all-gather.11.cloned.1.call-start = ((), (), s32[]{:S(2)}) async-start(), calls=%async_computation.2 | async-start | bytes 4608000 | tf_op jit(solution)/shard_map/all_gather | solution.py:23
  542.9 289.3 %all-gather.7.cloned.1.call-start = ((), (), s32[]{:S(2)}) async-start(), calls=%async_computation | async-start | bytes 4608000 | tf_op jit(solution)/shard_map/all_gather | solution.py:23
  698.2 5.2 copy-start.6
  709.8 6.7 copy-start.4
  712.4 135.7 %collective-permute-start.3 = (f32[1000,512]{1,0:T(8,128)}, f32[1000,512]{1,0:T(8,128)}, u32[]{:S(2)}, u32[]{:S(2)}) collective-permute-start(f32[1000,512]{1,0:T(8,128)} %fusion.1), channel_id=1, source_target_pairs={{16,0},{24,8},{32,16},{40,24},{48,32},{56,40},{64,48},{72,56},{80,... | collective-permute-start | bytes 6144008 | tf_op jit(solution)/shard_map/ppermute | solution.py:12
  719.1 129.0 %collective-permute-start.2 = (f32[1000,512]{1,0:T(8,128)}, f32[1000,512]{1,0:T(8,128)}, u32[]{:S(2)}, u32[]{:S(2)}) collective-permute-start(f32[1000,512]{1,0:T(8,128)} %fusion.3), channel_id=1, source_target_pairs={{8,0},{16,8},{24,16},{32,24},{40,32},{48,40},{56,48},{64,56},{72,6... | collective-permute-start | bytes 6144008 | tf_op jit(solution)/shard_map/ppermute | solution.py:12
  842.2 3.2 copy-start.3
  845.4 2.7 copy-start.2
Sparse Core Ops, SparseCore 0:
  44.7 493.5 all-reduce.5
  541.0 76.0 all-gather.8
  619.7 73.5 all-gather.10
  695.8 136.3 all-gather.6
where the time goes:
time: 862 us; the launch traced here: 860 us
  waiting for transfers between devices  768 us (89%)
  local copies, waits for them, and re-layouts  39.6 us (5%)
  matrix products  27.5 us (3%)
  between operations  13.9 us (2%)
    unnamed x5, waiting for transfers between devices  492 us
    all_gather x3, waiting for transfers between devices, amplitudes(): k_full = lax.all_gather(k_rows, 'aux', axis=0, tiled=True)  250 us
    ppermute x4, waiting for transfers between devices, passed_along(): return lax.ppermute(block, axis, route)  25.6 us
    unnamed x25, local copies, waits for them, and re-layouts  24.3 us
  transfers between devices with their start and end apart: 8, of which 6 were waited for; matrix products, arithmetic and copies ran while one was open for 7% of the time, Pallas kernels for 0%

commit v1 on v0

v1 whole, which is shorter than its diff:
```python
import functools

import jax
import jax.numpy as jnp
from jax import lax
from jax.experimental import pallas as pl
from jax.experimental.pallas import tpu as pltpu
from jax.sharding import PartitionSpec as P

MESH = pl.DeviceIdType.MESH
PAD = 1024
BLOCK = 128
HALF = 512
F32 = jnp.float32
BF16 = jnp.bfloat16


def kernel(
    n_occ, b_ref, occ_ref, vrow_ref, vcol_ref, g_ref,
    nb, kp, kr, am, rsend, rrecv,
    b_ss, b_rs, k_ss, k_rs, a_ss, a_rs, r_ss, r_rs,
):
    occ = lax.axis_index("occ")
    aux = lax.axis_index("aux")
    core = lax.rem(occ, 2)
    y = lax.div(aux, 2)
    h = lax.rem(aux, 2)
    mine = h * 4 + y

    def orbital(d):
        return lax.rem(occ + d + n_occ, n_occ)

    def peer(d):
        dh, dy = d // 4, d % 4
        py, ph = lax.rem(y + dy, 4), lax.rem(h + dh, 2)
        return (occ, py * 2 + ph), ph * 4 + py

    j1 = orbital(-1 - core)
    j2 = orbital(2 - 3 * core)
    to_a = orbital(-2 + 3 * core)
    to_b = orbital(1 + core)
    peers = [peer(d) for d in range(1, 8)]

    barrier = pltpu.get_barrier_semaphore()
    greeted = [dev for dev, _ in peers] + [(j1, aux), (j2, aux), (to_a, aux), (to_b, aux)]
    for dev in greeted:
        pl.semaphore_signal(barrier, inc=1, device_id=dev, device_id_type=MESH)
    pl.semaphore_wait(barrier, len(greeted))

    def remote(src, dst, ss, rs, dev):
        return pltpu.make_async_remote_copy(
            src_ref=src, dst_ref=dst, send_sem=ss, recv_sem=rs, device_id=dev, device_id_type=MESH
        )

    slot = 1 - core
    b_copies = [
        remote(b_ref, nb.at[slot], b_ss.at[n], b_rs.at[slot], (dev, aux))
        for n, dev in enumerate((to_a, to_b))
    ]
    for c in b_copies:
        c.start()

    def rows(block):
        return pl.ds(pl.multiple_of(block * BLOCK, BLOCK), BLOCK)

    def partial_k(k, right):
        @pl.loop(0, 8)
        def _(t):
            r = pl.ds(pl.multiple_of((t // 4) * HALF, HALF), HALF)
            cc = pl.ds(pl.multiple_of((t % 4) * 256, 256), 256)
            part = lax.dot_general(
                b_ref[r, :], right[cc, :], (((1,), (1,)), ((), ())), preferred_element_type=F32
            )
            kp[k, r, cc] = part.astype(BF16)

        copies = []
        for n, (dev, block) in enumerate(peers):
            c = remote(kp.at[k, rows(block)], kr.at[k, rows(mine)], k_ss.at[k, n], k_rs.at[k, mine], dev)
            c.start()
            copies.append(c)
        return copies

    def arrive(k, buf, sems, block, dev):
        remote(buf.at[k, rows(block)], buf.at[k, rows(block)], sems.at[k, block], sems.at[k, block], dev).wait_recv()

    e_mine = occ_ref[occ]

    def amplitude(k, e_other):
        for dev, block in peers:
            arrive(k, kr, k_rs, block, dev)

        @pl.loop(0, 8)
        def _(t):
            lo = t * 16
            total = kp[k, pl.ds(pl.multiple_of(mine * BLOCK + lo, 16), 16), :].astype(F32)
            for _, block in peers:
                total += kr[k, pl.ds(pl.multiple_of(block * BLOCK + lo, 16), 16), :].astype(F32)
            va = vcol_ref[pl.ds(pl.multiple_of(mine * BLOCK + lo, 16), 16), :]
            denom = va + vrow_ref[...] - e_mine - e_other
            am[k, pl.ds(pl.multiple_of(mine * BLOCK + lo, 16), 16), :] = (total / denom).astype(BF16)

        copies = []
        for n, (dev, block) in enumerate(peers):
            c = remote(am.at[k, rows(mine)], am.at[k, rows(mine)], a_ss.at[k, n], a_rs.at[k, mine], dev)
            c.start()
            copies.append(c)
        return copies

    def gather(k):
        for dev, block in peers:
            arrive(k, am, a_rs, block, dev)

    def add_gamma(k, right, first):
        @pl.loop(0, 4)
        def _(t):
            r = pl.ds(pl.multiple_of((t // 2) * HALF, HALF), HALF)
            cc = pl.ds(pl.multiple_of((t % 2) * 256, 256), 256)
            term = jnp.dot(am[k, r, :], right[:, cc], preferred_element_type=F32)
            if first:
                g_ref[r, cc] = term
            else:
                g_ref[r, cc] += term

    def give_back(k, n, dev):
        @pl.loop(0, 4)
        def _(t):
            r = pl.ds(pl.multiple_of((t // 2) * HALF, HALF), HALF)
            cc = pl.ds(pl.multiple_of((t % 2) * 256, 256), 256)
            term = lax.dot_general(
                am[k, :, r], b_ref[:, cc], (((0,), (0,)), ((), ())), preferred_element_type=F32
            )
            rsend[n, r, cc] = term.astype(BF16)

        c = remote(rsend.at[n], rrecv.at[core], r_ss.at[n], r_rs.at[core], (dev, aux))
        c.start()
        return c

    sent = []
    sent += partial_k(0, b_ref)
    remote(b_ref, nb.at[1], b_ss.at[1], b_rs.at[1], (j2, aux)).wait_recv()
    sent += partial_k(2, nb.at[1])
    remote(b_ref, nb.at[0], b_ss.at[0], b_rs.at[0], (j1, aux)).wait_recv()
    sent += partial_k(1, nb.at[0])
    sent += amplitude(0, e_mine)
    sent += amplitude(2, occ_ref[j2])
    sent += amplitude(1, occ_ref[j1])
    gather(0)
    add_gamma(0, b_ref, True)
    gather(2)
    r2 = give_back(2, 1, j2)
    add_gamma(2, nb.at[1], False)
    gather(1)
    r1 = give_back(1, 0, j1)
    add_gamma(1, nb.at[0], False)
    for c in b_copies:
        c.wait_send()
    for c in sent:
        c.wait_send()
    r2.wait_send()
    r1.wait_send()
    for n in range(2):
        remote(rsend.at[n], rrecv.at[n], r_ss.at[n], r_rs.at[n], (to_a, aux)).wait_recv()

    @pl.loop(0, 8)
    def _(t):
        r = pl.ds(pl.multiple_of(t * BLOCK, BLOCK), BLOCK)
        g_ref[r, :] += rrecv[0, r, :].astype(F32) + rrecv[1, r, :].astype(F32)


def local(n_occ, three_index, occ_energy, vir_energy):
    v = three_index.shape[1]
    b = jnp.pad(three_index[0], ((0, PAD - v), (0, 0)))
    vir = jnp.pad(vir_energy, (0, PAD - v), constant_values=1.0)
    width = b.shape[1]
    vmem = pl.BlockSpec(memory_space=pltpu.VMEM)
    dma = pltpu.SemaphoreType.DMA
    gamma = pl.pallas_call(
        functools.partial(kernel, n_occ),
        out_shape=jax.ShapeDtypeStruct((PAD, width), F32),
        in_specs=[vmem, pl.BlockSpec(memory_space=pltpu.SMEM), vmem, vmem],
        out_specs=vmem,
        scratch_shapes=[
            pltpu.VMEM((2, PAD, width), BF16),
            pltpu.VMEM((3, PAD, PAD), BF16),
            pltpu.VMEM((3, PAD, PAD), BF16),
            pltpu.VMEM((3, PAD, PAD), BF16),
            pltpu.VMEM((2, PAD, width), BF16),
            pltpu.VMEM((2, PAD, width), BF16),
            dma((2,)), dma((2,)),
            dma((3, 7)), dma((3, 8)),
            dma((3, 7)), dma((3, 8)),
            dma((2,)), dma((2,)),
        ],
        compiler_params=pltpu.CompilerParams(
            collective_id=0, has_side_effects=True, vmem_limit_bytes=56 * 2**20
        ),
        cost_estimate=pl.CostEstimate(flops=8 * 10**9, bytes_accessed=4 * 10**6, transcendentals=0),
    )(b, occ_energy, vir[None, :], vir[:, None])
    return gamma[None, :v]


def solution(mesh):
    placed = (P("occ", None, "aux"), P(), P())
    return jax.shard_map(
        functools.partial(local, mesh.shape["occ"]),
        mesh=mesh, in_specs=placed, out_specs=P("occ", None, "aux"), check_vma=False,
    )
```

time: 862 us -> 217 us (0.25)
  waiting for transfers between devices: 768 us -> 0 us
  Pallas kernels: 0 us -> 210 us
  local copies, waits for them, and re-layouts: 39.6 us -> 7.01 us
  matrix products: 27.5 us -> 0 us
  between operations: 13.9 us -> 0.01 us
    unnamed x5 -> x0, waiting for transfers between devices: 492 us -> none
    all_gather x3 -> x0, waiting for transfers between devices: 250 us -> none  [amplitudes(): k_full = lax.all_gather(k_rows, 'aux', axis=0, tiled=True)]
    pallas_call x0 -> x1, Pallas kernels: none -> 210 us  [local(): pl.pallas_call(functools.partial(kernel, n_occ), out_shape=jax.ShapeDtype...]
    dot_general x8 -> x0, matrix products: 27.5 us -> none  [the longest x3 11.5 us: pair_product(): lax.dot_general(left, right, (((1,), (1,)), ((), ())), preferred_element_...]
    ppermute x4 -> x0, waiting for transfers between devices: 25.6 us -> none  [passed_along(): return lax.ppermute(block, axis, route)]
    unnamed x25 -> x2, local copies, waits for them, and re-layouts: 24.3 us -> 0.01 us
    all_gather x3 -> x0, local copies, waits for them, and re-layouts: 14.6 us -> none  [amplitudes(): k_full = lax.all_gather(k_rows, 'aux', axis=0, tiled=True)]
  transfers between devices with their start and end apart: 8 -> 0, of which waited for: 6 -> 0; matrix products, arithmetic and copies ran while one was open for 7% -> 0% of each run, Pallas kernels for 0% -> 0%
where the time goes in v1:
time: 217 us
  Pallas kernels  210 us (97%)
  local copies, waits for them, and re-layouts  7.01 us (3%)
    pallas_call x1, Pallas kernels, local(): pl.pallas_call(functools.partial(kernel, n_occ), out_shape=jax.ShapeDtype...  210 us

profile of v1, /device:TPU:2, one launch (start us, length us, event | category | flops | bytes accessed | tf_op | source)
XLA Modules:
  0.0 216.8 jit_solution(5091882795912883913)
XLA Ops:
  0.0 0.7 pad.9
  0.7 0.0 copy-start
  0.7 1.0 copy.4.vcol_ref
  1.7 2.3 %pad.8.b_ref = bf16[1024,512]{1,0:T(8,128)(2,1)} pad(bf16[1000,512]{1,0:T(8,128)(2,1)} %bitcast.5, bf16[]{:T(256)} %constant.1.clone.1), padding=0_24x0_0 | pad | bytes 2072578 | tf_op jit(solution)/shard_map/jit(_pad)/pad | solution.py:172
  4.0 0.0 copy-done
  4.0 209.8 %shard_map.37 = f32[1024,512]{1,0:T(8,128)} custom-call(bf16[1024,512]{1,0:T(8,128)(2,1)} %pad.8.b_ref, f32[32]{0:T(128)} %occ_ref.1, f32[1,1024]{1,0:T(1,128)} %bitcast.7, f32[1024,1]{1,0:T(8,128)} %copy.4.vcol_ref), custom_call_target="tpu_custom_call" | custom-call | flops 8000000000 | bytes 4000000 | tf_op jit(solution)/shard_map/pallas_call | solution.py:177
  213.8 3.0 %slice_bitcast_fusion = f32[1,1000,512]{2,1,0:T(8,128)} fusion(f32[1024,512]{1,0:T(8,128)} %shard_map.37), kind=kLoop, calls=%fused_computation | loop fusion | bytes 4096000 | tf_op jit(solution)/shard_map/broadcast_in_dim | solution.py:199
Async XLA Ops:
  0.7 3.3 %copy-start = (f32[1024]{0:T(1024)}, f32[1024]{0:T(1024)S(1)}, u32[]{:S(2)}) copy-start(f32[1024]{0:T(1024)S(1)} %pad.9) | copy-start | bytes 12292

commit v2 on v0

v2 whole, which is shorter than its diff:
```python
import functools

import jax
import jax.numpy as jnp
from jax import lax
from jax.experimental import pallas as pl
from jax.experimental.pallas import tpu as pltpu
from jax.sharding import PartitionSpec as P

MESH = pl.DeviceIdType.MESH
PAD = 1024
BLOCK = 128
HALF = 512
SPLIT = 512
F32 = jnp.float32
BF16 = jnp.bfloat16


def kernel(
    n_occ, b_ref, occ_ref, vrow_ref, vcol_ref, g_ref,
    bp, nbo, nbp, kf, kp, kr, am, ret, rchip, rz,
    x_ss, x_rs, z_ss, z_rs, c_ss, c_rs, k_ss, k_rs, a_ss, a_rs, r_ss, r_rs,
):
    occ = lax.axis_index("occ")
    aux = lax.axis_index("aux")
    core = lax.rem(occ, 2)
    y = lax.div(aux, 2)
    h = lax.rem(aux, 2)
    o = 1 - h
    yp, ym, yy = lax.rem(y + 1, 4), lax.rem(y + 3, 4), lax.rem(y + 2, 4)

    def orbital(d):
        return lax.rem(occ + d + n_occ, n_occ)

    across = (occ, y * 2 + o)
    up, down, far = [(occ, q * 2 + h) for q in (yp, ym, yy)]
    sibling = (occ + 1 - 2 * core, aux)
    z_out = (orbital(4 * core - 2), aux)
    z_in = (orbital(2 - 4 * core), aux)
    zs, cs = 1 - core, core
    e_mine = occ_ref[occ]
    e_pair = (e_mine, occ_ref[orbital(-1 - core)], occ_ref[orbital(2 - 3 * core)])

    barrier = pltpu.get_barrier_semaphore()
    greeted = (across, up, down, far, sibling, z_out, z_in)
    for dev in greeted:
        pl.semaphore_signal(barrier, inc=1, device_id=dev, device_id_type=MESH)
    pl.semaphore_wait(barrier, len(greeted))

    def remote(src, dst, ss, rs, dev):
        return pltpu.make_async_remote_copy(
            src_ref=src, dst_ref=dst, send_sem=ss, recv_sem=rs, device_id=dev, device_id_type=MESH
        )

    sent = []

    def push(*args):
        c = remote(*args)
        c.start()
        sent.append(c)

    def ds(start, size):
        return pl.ds(pl.multiple_of(start, size), size)

    rows_h, rows_o = ds(h * HALF, HALF), ds(o * HALF, HALF)

    push(b_ref.at[rows_o, :], bp.at[rows_o, :], x_ss.at[0], x_rs.at[0], across)
    push(b_ref.at[rows_h, :], bp.at[rows_h, :], x_ss.at[1], x_rs.at[1], across)

    def b_part(n, source):
        if source is None:
            return (b_ref.at[rows_h, :], bp.at[rows_h, :], b_ref.at[rows_o, :])[n]
        return (nbo.at[source, rows_h, :], nbp.at[source], nbo.at[source, rows_o, :])[n]

    def z_send(n):
        push(b_part(n, None), b_part(n, zs), z_ss.at[n], z_rs.at[n], z_out)

    def chip_send(n, source):
        remote(b_part(n, source), b_part(n, 1 - core), c_ss.at[n], c_rs.at[n], sibling).start()

    def z_arrive(n):
        remote(b_part(n, zs), b_part(n, zs), z_ss.at[n], z_rs.at[n], z_in).wait_recv()

    def chip_arrive(n):
        remote(b_part(n, cs), b_part(n, cs), c_ss.at[n], c_rs.at[n], sibling).wait_recv()

    def own_to_chip(n):
        @pl.when(core == 0)
        def _():
            chip_send(n, None)

    def slot_to_chip(n):
        z_arrive(n)

        @pl.when(core == 1)
        def _():
            chip_send(n, 0)

    def partial_k(k, ab):
        c = o if ab else h
        cols = ds(c * HALF, HALF)
        left, left_p = (b_ref[rows_h, :], bp[rows_h, :]) if k == 0 else (nbo[k - 1, rows_h, :], nbp[k - 1])
        contract = (((1,), (1,)), ((), ()))
        part = lax.dot_general(left, b_ref[cols, :], contract, preferred_element_type=F32)
        part += lax.dot_general(left_p, bp[cols, :], contract, preferred_element_type=F32)
        kf[k, :, cols] = part
        kp[k, :, cols] = part.astype(BF16)
        for n, (q, dev) in enumerate(((yp, up), (ym, down), (yy, far))):
            push(
                kp.at[k, ds(q * BLOCK, BLOCK), cols], kr.at[k, ds(y * BLOCK, BLOCK), cols],
                k_ss.at[k, ab, n], k_rs.at[k, ab, y], dev,
            )

    base = h * HALF + y * BLOCK

    def amplitude(k):
        for ab in range(2):
            cols = ds((o if ab else h) * HALF, HALF)
            for q, dev in ((yp, up), (ym, down), (yy, far)):
                ref = kr.at[k, ds(q * BLOCK, BLOCK), cols]
                remote(ref, ref, k_rs.at[k, ab, q], k_rs.at[k, ab, q], dev).wait_recv()

        @pl.loop(0, 4)
        def _(t):
            total = kf[k, ds(y * BLOCK + t * 32, 32), :]
            for q in (yp, ym, yy):
                total += kr[k, ds(q * BLOCK + t * 32, 32), :].astype(F32)
            mine = ds(base + t * 32, 32)
            denom = vcol_ref[mine, :] + vrow_ref[...] - e_mine - e_pair[k]
            am[k, mine, :] = (total / denom).astype(BF16)

    first_cols, last_cols = pl.ds(0, SPLIT), pl.ds(SPLIT, PAD - SPLIT)
    all_cols = pl.ds(0, PAD)

    def piece(k, n):
        q, low = ((ym, 0), (yp, 0), (yy, 0), (yy, 64), (y, 0), (ym, 0), (yp, 0), (yy, 0), (yy, 64), (ym, 0), (yp, 0), (yy, 0))[n]
        side = h if n < 4 else o
        count = 64 if n in (2, 3, 7, 8) else BLOCK
        cols = all_cols if n < 5 else first_cols if n < 9 else last_cols
        return am.at[k, ds(side * HALF + q * BLOCK + low, count), cols]

    def gather_from(k, n):
        dev = (down, up, down, up, across, down, up, down, up, across, across, across)[n]
        remote(piece(k, n), piece(k, n), a_ss.at[k, n], a_rs.at[k, n], dev).wait_recv()

    def spread(k, n, side, q, low, count, cols, dev):
        ref = am.at[k, ds(side * HALF + q * BLOCK + low, count), cols]
        push(ref, ref, a_ss.at[k, n], a_rs.at[k, n], dev)

    def stage1(k):
        spread(k, 4, h, y, 0, BLOCK, all_cols, across)
        spread(k, 0, h, y, 0, BLOCK, all_cols, up)
        spread(k, 1, h, y, 0, BLOCK, all_cols, down)

    def stage2(k):
        gather_from(k, 0)
        spread(k, 2, h, ym, 0, 64, all_cols, up)
        spread(k, 9, h, ym, 0, BLOCK, last_cols, across)
        gather_from(k, 1)
        spread(k, 3, h, yp, 64, 64, all_cols, down)
        spread(k, 10, h, yp, 0, BLOCK, last_cols, across)
        gather_from(k, 4)
        spread(k, 5, o, y, 0, BLOCK, first_cols, up)
        spread(k, 6, o, y, 0, BLOCK, first_cols, down)

    def stage3(k):
        gather_from(k, 2)
        gather_from(k, 3)
        spread(k, 11, h, yy, 0, BLOCK, last_cols, across)
        gather_from(k, 5)
        spread(k, 7, o, ym, 0, 64, first_cols, up)
        gather_from(k, 6)
        spread(k, 8, o, yp, 64, 64, first_cols, down)

    def stage4(k):
        for n in (7, 8, 9, 10, 11):
            gather_from(k, n)

    def product(k, transposed, right, store):
        @pl.loop(0, 2)
        def _(t):
            r = ds(t * HALF, HALF)
            if transposed:
                term = lax.dot_general(am[k, :, r], right, (((0,), (0,)), ((), ())), preferred_element_type=F32)
            else:
                term = jnp.dot(am[k, r, :], right, preferred_element_type=F32)
            store(r, term)

    def set_gamma(r, term):
        g_ref[r, :] = term

    def add_gamma(r, term):
        g_ref[r, :] += term

    def set_return(n):
        def store(r, term):
            ret[n, r, :] = term.astype(BF16)

        return store

    z_send(0)
    own_to_chip(0)
    slot_to_chip(0)
    remote(bp.at[rows_h, :], bp.at[rows_h, :], x_ss.at[0], x_rs.at[0], across).wait_recv()
    z_send(1)
    own_to_chip(1)
    partial_k(0, 0)
    z_send(2)
    own_to_chip(2)
    slot_to_chip(1)
    chip_arrive(0)
    chip_arrive(1)
    partial_k(2, 0)
    partial_k(1, 0)
    remote(bp.at[rows_o, :], bp.at[rows_o, :], x_ss.at[1], x_rs.at[1], across).wait_recv()
    partial_k(1, 1)
    partial_k(2, 1)
    partial_k(0, 1)
    slot_to_chip(2)
    amplitude(1)
    stage1(1)
    amplitude(2)
    stage1(2)
    stage2(1)
    amplitude(0)
    stage1(0)
    stage2(2)
    stage3(1)
    stage2(0)
    stage3(2)
    chip_arrive(2)

    def return_to(n, dev, dst, m):
        return remote(ret.at[n], dst, r_ss.at[m], r_rs.at[m], dev)

    stage4(1)
    product(1, False, b_ref[...], set_return(0))

    @pl.when(core == 0)
    def _():
        return_to(0, sibling, rchip, 0).start()

    product(1, True, nbo[0], set_gamma)

    @pl.when(core == 1)
    def _():
        return_to(0, sibling, rchip, 0).wait_recv()

        @pl.loop(0, 8)
        def _(t):
            r = ds(t * BLOCK, BLOCK)
            ret[0, r, :] = (ret[0, r, :].astype(F32) + rchip[r, :].astype(F32)).astype(BF16)

        return_to(0, z_in, rz, 1).start()

    stage3(0)
    stage4(2)
    product(2, False, b_ref[...], set_return(1))

    @pl.when(core == 0)
    def _():
        return_to(1, z_in, rz, 1).start()

    @pl.when(core == 1)
    def _():
        return_to(1, sibling, rchip, 0).start()

    product(2, True, nbo[1], add_gamma)
    stage4(0)
    product(0, False, b_ref[...], add_gamma)
    return_to(1, z_out, rz, 1).wait_recv()

    @pl.loop(0, 8)
    def _(t):
        r = ds(t * BLOCK, BLOCK)
        g_ref[r, :] += rz[r, :].astype(F32)

    @pl.when(core == 0)
    def _():
        return_to(1, sibling, rchip, 0).wait_recv()

        @pl.loop(0, 8)
        def _(t):
            r = ds(t * BLOCK, BLOCK)
            g_ref[r, :] += rchip[r, :].astype(F32)

    for c in sent:
        c.wait_send()
    for n in range(3):
        remote(b_part(n, cs), b_part(n, cs), c_ss.at[n], c_rs.at[n], sibling).wait_send()
    for m in range(2):
        return_to(0, sibling, rchip, m).wait_send()


def local(n_occ, three_index, occ_energy, vir_energy):
    v = three_index.shape[1]
    b = jnp.pad(three_index[0], ((0, PAD - v), (0, 0)))
    vir = jnp.pad(vir_energy, (0, PAD - v), constant_values=1.0)
    width = b.shape[1]
    vmem = pl.BlockSpec(memory_space=pltpu.VMEM)
    dma = pltpu.SemaphoreType.DMA
    gamma = pl.pallas_call(
        functools.partial(kernel, n_occ),
        out_shape=jax.ShapeDtypeStruct((PAD, width), F32),
        in_specs=[vmem, pl.BlockSpec(memory_space=pltpu.SMEM), vmem, vmem],
        out_specs=vmem,
        scratch_shapes=[
            pltpu.VMEM((PAD, width), BF16),
            pltpu.VMEM((2, PAD, width), BF16),
            pltpu.VMEM((2, HALF, width), BF16),
            pltpu.VMEM((3, HALF, PAD), F32),
            pltpu.VMEM((3, HALF, PAD), BF16),
            pltpu.VMEM((3, HALF, PAD), BF16),
            pltpu.VMEM((3, PAD, PAD), BF16),
            pltpu.VMEM((2, PAD, width), BF16),
            pltpu.VMEM((PAD, width), BF16),
            pltpu.VMEM((PAD, width), BF16),
            dma((2,)), dma((2,)),
            dma((3,)), dma((3,)),
            dma((3,)), dma((3,)),
            dma((3, 2, 3)), dma((3, 2, 4)),
            dma((3, 12)), dma((3, 12)),
            dma((2,)), dma((2,)),
        ],
        compiler_params=pltpu.CompilerParams(
            collective_id=0, has_side_effects=True, vmem_limit_bytes=56 * 2**20
        ),
        cost_estimate=pl.CostEstimate(flops=8 * 10**9, bytes_accessed=4 * 10**6, transcendentals=0),
    )(b, occ_energy, vir[None, :], vir[:, None])
    return gamma[None, :v]


def solution(mesh):
    placed = (P("occ", None, "aux"), P(), P())
    return jax.shard_map(
        functools.partial(local, mesh.shape["occ"]),
        mesh=mesh, in_specs=placed, out_specs=P("occ", None, "aux"), check_vma=False,
    )
```

time: 862 us -> 134 us (0.16)
  waiting for transfers between devices: 768 us -> 0 us
  Pallas kernels: 0 us -> 126 us
  local copies, waits for them, and re-layouts: 39.6 us -> 7.01 us
  matrix products: 27.5 us -> 0 us
  between operations: 13.9 us -> 0.01 us
    unnamed x5 -> x0, waiting for transfers between devices: 492 us -> none
    all_gather x3 -> x0, waiting for transfers between devices: 250 us -> none  [amplitudes(): k_full = lax.all_gather(k_rows, 'aux', axis=0, tiled=True)]
    pallas_call x0 -> x1, Pallas kernels: none -> 126 us  [local(): pl.pallas_call(functools.partial(kernel, n_occ), out_shape=jax.ShapeDtype...]
    dot_general x8 -> x0, matrix products: 27.5 us -> none  [the longest x3 11.5 us: pair_product(): lax.dot_general(left, right, (((1,), (1,)), ((), ())), preferred_element_...]
    ppermute x4 -> x0, waiting for transfers between devices: 25.6 us -> none  [passed_along(): return lax.ppermute(block, axis, route)]
    unnamed x25 -> x2, local copies, waits for them, and re-layouts: 24.3 us -> 0.01 us
    all_gather x3 -> x0, local copies, waits for them, and re-layouts: 14.6 us -> none  [amplitudes(): k_full = lax.all_gather(k_rows, 'aux', axis=0, tiled=True)]
  transfers between devices with their start and end apart: 8 -> 0, of which waited for: 6 -> 0; matrix products, arithmetic and copies ran while one was open for 7% -> 0% of each run, Pallas kernels for 0% -> 0%
where the time goes in v2:
time: 134 us; the launch traced here: 133 us
  Pallas kernels  126 us (94%)
  local copies, waits for them, and re-layouts  7.01 us (5%)
    pallas_call x1, Pallas kernels, local(): pl.pallas_call(functools.partial(kernel, n_occ), out_shape=jax.ShapeDtype...  126 us
    broadcast_in_dim x1, local copies, waits for them, and re-layouts, local(): return gamma[None, :v]  3.04 us

profile of v2, /device:TPU:2, one launch (start us, length us, event | category | flops | bytes accessed | tf_op | source)
XLA Modules:
  0.0 132.6 jit_solution(7065928822774817152)
XLA Ops:
  0.0 0.7 pad.9
  0.7 0.0 copy-start
  0.7 1.0 copy.4.vcol_ref
  1.7 2.3 %pad.8.b_ref = bf16[1024,512]{1,0:T(8,128)(2,1)} pad(bf16[1000,512]{1,0:T(8,128)(2,1)} %bitcast.5, bf16[]{:T(256)} %constant.1.clone.1), padding=0_24x0_0 | pad | bytes 2072578 | tf_op jit(solution)/shard_map/jit(_pad)/pad | solution.py:297
  4.0 0.0 copy-done
  4.0 125.6 %shard_map.37 = f32[1024,512]{1,0:T(8,128)} custom-call(bf16[1024,512]{1,0:T(8,128)(2,1)} %pad.8.b_ref, f32[32]{0:T(128)} %occ_ref.1, f32[1,1024]{1,0:T(1,128)} %bitcast.7, f32[1024,1]{1,0:T(8,128)} %copy.4.vcol_ref), custom_call_target="tpu_custom_call" | custom-call | flops 8000000000 | bytes 4000000 | tf_op jit(solution)/shard_map/pallas_call | solution.py:302
  129.6 3.0 %slice_bitcast_fusion = f32[1,1000,512]{2,1,0:T(8,128)} fusion(f32[1024,512]{1,0:T(8,128)} %shard_map.37), kind=kLoop, calls=%fused_computation | loop fusion | bytes 4096000 | tf_op jit(solution)/shard_map/broadcast_in_dim | solution.py:330
Async XLA Ops:
  0.7 3.3 %copy-start = (f32[1024]{0:T(1024)}, f32[1024]{0:T(1024)S(1)}, u32[]{:S(2)}) copy-start(f32[1024]{0:T(1024)S(1)} %pad.9) | copy-start | bytes 12292

commit v3 on v2

v3 whole, which is shorter than its diff:
```python
import functools

import jax
import jax.numpy as jnp
from jax import lax
from jax.experimental import pallas as pl
from jax.experimental.pallas import tpu as pltpu
from jax.sharding import PartitionSpec as P

MESH = pl.DeviceIdType.MESH
PAD = 1024
BLOCK = 128
HALF = 512
SPLITS = (512, 640)
SPLITS_SELF = (384, 512)
SELF_COLS = 768
F32 = jnp.float32
BF16 = jnp.bfloat16


def kernel(
    n_occ, b_in, occ_ref, vir_ref, g_ref,
    b_ref, vrow, vcol, bp, nbo, nbp, kf, kp, kr, am, ret, rchip, rz,
    x_ss, x_rs, z_ss, z_rs, c_ss, c_rs, k_ss, k_rs, a_ss, a_rs, r_ss, r_rs,
):
    occ = lax.axis_index("occ")
    aux = lax.axis_index("aux")
    core = lax.rem(occ, 2)
    y = lax.div(aux, 2)
    h = lax.rem(aux, 2)
    o = 1 - h
    z = lax.rem(lax.div(occ, 2), 8)
    crowded = z * (7 - z) == 0
    yp, ym, yy = lax.rem(y + 1, 4), lax.rem(y + 3, 4), lax.rem(y + 2, 4)

    def orbital(d):
        return lax.rem(occ + d + n_occ, n_occ)

    across = (occ, y * 2 + o)
    up, down, far = [(occ, q * 2 + h) for q in (yp, ym, yy)]
    sibling = (occ + 1 - 2 * core, aux)
    z_out = (orbital(4 * core - 2), aux)
    z_in = (orbital(2 - 4 * core), aux)
    zs, cs = 1 - core, core
    e_mine = occ_ref[occ]
    e_pair = (e_mine, occ_ref[orbital(-1 - core)], occ_ref[orbital(2 - 3 * core)])

    barrier = pltpu.get_barrier_semaphore()
    greeted = (across, up, down, far, sibling, z_out, z_in)
    for dev in greeted:
        pl.semaphore_signal(barrier, inc=1, device_id=dev, device_id_type=MESH)

    v = b_in.shape[0]
    whole = v // 16 * 16
    b_ref[:whole, :] = b_in[:whole, :]
    tail = jnp.zeros((PAD - v, b_in.shape[1]), F32)
    b_ref[whole:, :] = jnp.concatenate([b_in[whole:, :].astype(F32), tail], axis=0).astype(BF16)
    vrow[...] = jnp.ones_like(vrow)
    vrow[:, :v] = vir_ref[...]
    base = pl.multiple_of(h * HALF + y * BLOCK, BLOCK)
    here = jnp.broadcast_to(vrow[:, pl.ds(base, BLOCK)], (BLOCK, BLOCK))
    diagonal = lax.broadcasted_iota(jnp.int32, (BLOCK, BLOCK), 0) == lax.broadcasted_iota(jnp.int32, (BLOCK, BLOCK), 1)
    vcol[...] = jnp.sum(jnp.where(diagonal, here, 0.0), axis=1, keepdims=True)
    pl.semaphore_wait(barrier, len(greeted))

    def remote(src, dst, ss, rs, dev):
        return pltpu.make_async_remote_copy(
            src_ref=src, dst_ref=dst, send_sem=ss, recv_sem=rs, device_id=dev, device_id_type=MESH
        )

    sent = []

    def push(*args):
        c = remote(*args)
        c.start()
        sent.append(c)

    def ds(start, size):
        return pl.ds(pl.multiple_of(start, size), size)

    rows_h, rows_o = ds(h * HALF, HALF), ds(o * HALF, HALF)

    push(b_ref.at[rows_o, :], bp.at[rows_o, :], x_ss.at[0], x_rs.at[0], across)

    def b_part(n, source):
        if source is None:
            return (b_ref.at[rows_h, :], bp.at[rows_h, :], b_ref.at[rows_o, :])[n]
        return (nbo.at[source, rows_h, :], nbp.at[source], nbo.at[source, rows_o, :])[n]

    def z_send(n):
        push(b_part(n, None), b_part(n, zs), z_ss.at[n], z_rs.at[n], z_out)

    def chip_send(n, source):
        remote(b_part(n, source), b_part(n, 1 - core), c_ss.at[n], c_rs.at[n], sibling).start()

    def z_arrive(n):
        remote(b_part(n, zs), b_part(n, zs), z_ss.at[n], z_rs.at[n], z_in).wait_recv()

    def chip_arrive(n):
        remote(b_part(n, cs), b_part(n, cs), c_ss.at[n], c_rs.at[n], sibling).wait_recv()

    def own_to_chip(n):
        @pl.when(core == 0)
        def _():
            chip_send(n, None)

    def slot_to_chip(n):
        z_arrive(n)

        @pl.when(core == 1)
        def _():
            chip_send(n, 0)

    def k_cols(k, ab):
        if k == 0:
            return pl.ds(HALF, 256) if ab else pl.ds(0, HALF)
        return ds((o if ab else h) * HALF, HALF)

    contract = (((1,), (1,)), ((), ()))

    def partial_k(k, ab):
        cols = k_cols(k, ab)
        if k == 0 and ab:
            for s in range(2):
                left = ds(h * HALF + s * 256, 256)
                right = ds(o * HALF + lax.rem(s + h, 2) * 256, 256)
                part = lax.dot_general(b_ref[left, :], b_ref[right, :], contract, preferred_element_type=F32)
                part += lax.dot_general(bp[left, :], bp[right, :], contract, preferred_element_type=F32)
                kf[k, pl.ds(s * 256, 256), cols] = part
                kp[k, pl.ds(s * 256, 256), cols] = part.astype(BF16)
        else:
            right = ds((o if ab else h) * HALF, HALF)
            left, left_p = (b_ref[rows_h, :], bp[rows_h, :]) if k == 0 else (nbo[k - 1, rows_h, :], nbp[k - 1])
            part = lax.dot_general(left, b_ref[right, :], contract, preferred_element_type=F32)
            part += lax.dot_general(left_p, bp[right, :], contract, preferred_element_type=F32)
            kf[k, :, cols] = part
            kp[k, :, cols] = part.astype(BF16)
        for n, (q, dev) in enumerate(((yp, up), (ym, down), (yy, far))):
            push(
                kp.at[k, ds(q * BLOCK, BLOCK), cols], kr.at[k, ds(y * BLOCK, BLOCK), cols],
                k_ss.at[k, ab, n], k_rs.at[k, ab, y], dev,
            )

    def amplitude(k):
        for ab in range(2):
            cols = k_cols(k, ab)
            for q, dev in ((yp, up), (ym, down), (yy, far)):
                ref = kr.at[k, ds(q * BLOCK, BLOCK), cols]
                remote(ref, ref, k_rs.at[k, ab, q], k_rs.at[k, ab, q], dev).wait_recv()
            energy = cols
            if k == 0:
                energy = ds(o * HALF + lax.rem(y // 2 + h, 2) * 256, 256) if ab else rows_h

            @pl.loop(0, 4)
            def _(t):
                total = kf[k, ds(y * BLOCK + t * 32, 32), cols]
                for q in (yp, ym, yy):
                    total += kr[k, ds(q * BLOCK + t * 32, 32), cols].astype(F32)
                denom = vcol[ds(t * 32, 32), :] + vrow[:, energy] - e_mine - e_pair[k]
                am[k, ds(base + t * 32, 32), cols] = (total / denom).astype(BF16)

    def piece(k, n, side, q, low, w):
        count = 64 if n in (2, 3, 7, 8) else BLOCK
        width = PAD if k else SELF_COLS
        split = (SPLITS if k else SPLITS_SELF)[w]
        cols = pl.ds(0, width) if n < 5 else pl.ds(0, split) if n < 9 else pl.ds(split, width - split)
        return am.at[k, ds(side * HALF + q * BLOCK + low, count), cols]

    def by_plane(f):
        pl.when(crowded)(lambda: f(1))
        pl.when(jnp.logical_not(crowded))(lambda: f(0))

    def spread(k, n, side, q, low, dev, w=0):
        ref = piece(k, n, side, q, low, w)
        remote(ref, ref, a_ss.at[k, n], a_rs.at[k, n], dev).start()

    def gather_from(k, n, w=0):
        q, low = ((ym, 0), (yp, 0), (yy, 0), (yy, 64), (y, 0), (ym, 0), (yp, 0), (yy, 0), (yy, 64), (ym, 0), (yp, 0), (yy, 0))[n]
        dev = (down, up, down, up, across, down, up, down, up, across, across, across)[n]
        ref = piece(k, n, h if n < 4 else o, q, low, w)
        remote(ref, ref, a_ss.at[k, n], a_rs.at[k, n], dev).wait_recv()

    def stage1(k):
        spread(k, 4, h, y, 0, across)
        spread(k, 0, h, y, 0, up)
        spread(k, 1, h, y, 0, down)

    def stage2(k):
        @by_plane
        def _(w):
            gather_from(k, 0)
            spread(k, 2, h, ym, 0, up)
            spread(k, 9, h, ym, 0, across, w)
            gather_from(k, 1)
            spread(k, 3, h, yp, 64, down)
            spread(k, 10, h, yp, 0, across, w)
            gather_from(k, 4)
            spread(k, 5, o, y, 0, up, w)
            spread(k, 6, o, y, 0, down, w)

    def stage3(k):
        @by_plane
        def _(w):
            gather_from(k, 2)
            gather_from(k, 3)
            spread(k, 11, h, yy, 0, across, w)
            gather_from(k, 5, w)
            spread(k, 7, o, ym, 0, up, w)
            gather_from(k, 6, w)
            spread(k, 8, o, yp, 64, down, w)

    def stage4(k):
        @by_plane
        def _(w):
            for n in (7, 8, 9, 10, 11):
                gather_from(k, n, w)

    def product(k, transposed, right, store):
        @pl.loop(0, 2)
        def _(t):
            r = ds(t * HALF, HALF)
            if transposed:
                term = lax.dot_general(am[k, :, r], right, (((0,), (0,)), ((), ())), preferred_element_type=F32)
            else:
                term = jnp.dot(am[k, r, :], right, preferred_element_type=F32)
            store(r, term)

    def set_gamma(r, term):
        g_ref[r, :] = term

    def add_gamma(r, term):
        g_ref[r, :] += term

    def set_return(n):
        def store(r, term):
            ret[n, r, :] = term.astype(BF16)

        return store

    def self_product():
        for side in range(2):
            r = pl.ds(side * HALF, HALF)
            g_ref[r, :] += jnp.dot(am[0, r, pl.ds(0, HALF)], b_ref[r, :], preferred_element_type=F32)
        for side in range(2):
            for s in range(2):
                r = pl.ds(side * HALF + s * 256, 256)
                c = pl.ds((1 - side) * HALF + (s + side) % 2 * 256, 256)
                block = am[0, r, pl.ds(HALF, 256)]
                g_ref[r, :] += jnp.dot(block, b_ref[c, :], preferred_element_type=F32)
                g_ref[c, :] += lax.dot_general(block, b_ref[r, :], (((0,), (0,)), ((), ())), preferred_element_type=F32)

    def return_part(n, half, dst, dev):
        rows = rows_o if half else rows_h
        m = 0 if dst is rchip else 1
        return remote(ret.at[n, rows, :], dst.at[rows, :], r_ss.at[m, half], r_rs.at[m, half], dev)

    def give_back(k, half):
        rows = rows_o if half else rows_h
        ret[k - 1, rows, :] = jnp.dot(am[k, rows, :], b_ref[...], preferred_element_type=F32).astype(BF16)

        @pl.when(core == k - 1)
        def _():
            return_part(k - 1, half, rchip, sibling).start()

        if k == 2:
            @pl.when(core == 0)
            def _():
                return_part(1, half, rz, z_in).start()

    def merge(half):
        rows = rows_o if half else rows_h

        @pl.when(core == 1)
        def _():
            return_part(0, half, rchip, sibling).wait_recv()
            ret[0, rows, :] = (ret[0, rows, :].astype(F32) + rchip[rows, :].astype(F32)).astype(BF16)
            return_part(0, half, rz, z_in).start()

    z_send(0)
    own_to_chip(0)
    slot_to_chip(0)
    remote(bp.at[rows_h, :], bp.at[rows_h, :], x_ss.at[0], x_rs.at[0], across).wait_recv()
    z_send(1)
    own_to_chip(1)
    push(b_ref.at[rows_h, :], bp.at[rows_h, :], x_ss.at[1], x_rs.at[1], across)
    partial_k(0, 0)
    slot_to_chip(1)
    chip_arrive(0)
    chip_arrive(1)
    partial_k(2, 0)
    partial_k(1, 0)
    remote(bp.at[rows_o, :], bp.at[rows_o, :], x_ss.at[1], x_rs.at[1], across).wait_recv()
    z_send(2)
    own_to_chip(2)
    partial_k(1, 1)
    partial_k(2, 1)
    partial_k(0, 1)
    amplitude(1)
    stage1(1)
    slot_to_chip(2)
    amplitude(2)
    stage1(2)
    stage2(1)
    amplitude(0)
    stage1(0)
    stage2(2)
    stage3(1)
    give_back(1, 0)
    merge(0)
    stage3(2)
    give_back(2, 0)
    stage2(0)
    chip_arrive(2)
    stage4(1)
    give_back(1, 1)
    product(1, True, nbo[0], set_gamma)
    merge(1)
    stage3(0)
    stage4(2)
    give_back(2, 1)
    product(2, True, nbo[1], add_gamma)
    stage4(0)
    self_product()
    for half in range(2):
        return_part(1, half, rz, z_out).wait_recv()

    @pl.loop(0, 8)
    def _(t):
        r = ds(t * BLOCK, BLOCK)
        g_ref[r, :] += rz[r, :].astype(F32)

    @pl.when(core == 0)
    def _():
        for half in range(2):
            return_part(1, half, rchip, sibling).wait_recv()

        @pl.loop(0, 8)
        def _(t):
            r = ds(t * BLOCK, BLOCK)
            g_ref[r, :] += rchip[r, :].astype(F32)

    for c in sent:
        c.wait_send()

    @by_plane
    def _(w):
        for k in range(3):
            for n in range(12):
                ref = piece(k, n, 0, 0, 0, w)
                remote(ref, ref, a_ss.at[k, n], a_rs.at[k, n], across).wait_send()

    for n in range(3):
        remote(b_part(n, cs), b_part(n, cs), c_ss.at[n], c_rs.at[n], sibling).wait_send()
    for half in range(2):
        return_part(0, half, rchip, sibling).wait_send()
        return_part(0, half, rz, z_in).wait_send()


def local(n_occ, three_index, occ_energy, vir_energy):
    v = three_index.shape[1]
    width = three_index.shape[2]
    vmem = pl.BlockSpec(memory_space=pltpu.VMEM)
    dma = pltpu.SemaphoreType.DMA
    gamma = pl.pallas_call(
        functools.partial(kernel, n_occ),
        out_shape=jax.ShapeDtypeStruct((PAD, width), F32),
        in_specs=[vmem, pl.BlockSpec(memory_space=pltpu.SMEM), vmem],
        out_specs=vmem,
        scratch_shapes=[
            pltpu.VMEM((PAD, width), BF16),
            pltpu.VMEM((1, PAD), F32),
            pltpu.VMEM((BLOCK, 1), F32),
            pltpu.VMEM((PAD, width), BF16),
            pltpu.VMEM((2, PAD, width), BF16),
            pltpu.VMEM((2, HALF, width), BF16),
            pltpu.VMEM((3, HALF, PAD), F32),
            pltpu.VMEM((3, HALF, PAD), BF16),
            pltpu.VMEM((3, HALF, PAD), BF16),
            pltpu.VMEM((3, PAD, PAD), BF16),
            pltpu.VMEM((2, PAD, width), BF16),
            pltpu.VMEM((PAD, width), BF16),
            pltpu.VMEM((PAD, width), BF16),
            dma((2,)), dma((2,)),
            dma((3,)), dma((3,)),
            dma((3,)), dma((3,)),
            dma((3, 2, 3)), dma((3, 2, 4)),
            dma((3, 12)), dma((3, 12)),
            dma((2, 2)), dma((2, 2)),
        ],
        compiler_params=pltpu.CompilerParams(
            collective_id=0, has_side_effects=True, vmem_limit_bytes=56 * 2**20
        ),
        cost_estimate=pl.CostEstimate(flops=8 * 10**9, bytes_accessed=4 * 10**6, transcendentals=0),
    )(three_index[0], occ_energy, vir_energy[None, :])
    return gamma[None, :v]


def solution(mesh):
    placed = (P("occ", None, "aux"), P(), P())
    return jax.shard_map(
        functools.partial(local, mesh.shape["occ"]),
        mesh=mesh, in_specs=placed, out_specs=P("occ", None, "aux"), check_vma=False,
    )
```

time: 134 us -> 119 us (0.89)
  Pallas kernels: 126 us -> 115 us
  local copies, waits for them, and re-layouts: 7.01 us -> 3.04 us
    pallas_call x1, Pallas kernels: 126 us -> 115 us  [local(): pl.pallas_call(functools.partial(kernel, n_occ), out_shape=jax.ShapeDtype...]
    pad x2 -> x0, local copies, waits for them, and re-layouts: 2.94 us -> none  [the longest x1 2.25 us: local(): b = jnp.pad(three_index[0], ((0, PAD - v), (0, 0)))]
where the time goes in v3:
time: 119 us; the launch traced here: 118 us
  Pallas kernels  115 us (97%)
  local copies, waits for them, and re-layouts  3.04 us (3%)
    pallas_call x1, Pallas kernels, local(): pl.pallas_call(functools.partial(kernel, n_occ), out_shape=jax.ShapeDtype...  115 us
    broadcast_in_dim x1, local copies, waits for them, and re-layouts, local(): return gamma[None, :v]  3.04 us

profile of v3, /device:TPU:2, one launch (start us, length us, event | category | flops | bytes accessed | tf_op | source)
XLA Modules:
  0.0 118.1 jit_solution(3727636553269615765)
XLA Ops:
  0.0 115.1 %shard_map.37 = f32[1024,512]{1,0:T(8,128)} custom-call(bf16[1000,512]{1,0:T(8,128)(2,1)} %bitcast.4, f32[32]{0:T(128)} %occ_ref.1, f32[1,1000]{1,0:T(1,128)} %bitcast.5), custom_call_target="tpu_custom_call" | custom-call | flops 8000000000 | bytes 4000000 | tf_op jit(solution)/shard_map/pallas_call | solution.py:364
  115.1 3.0 %slice_bitcast_fusion = f32[1,1000,512]{2,1,0:T(8,128)} fusion(f32[1024,512]{1,0:T(8,128)} %shard_map.37), kind=kLoop, calls=%fused_computation | loop fusion | bytes 4096000 | tf_op jit(solution)/shard_map/broadcast_in_dim | solution.py:395

commit v4 on v3

--- a/solution.py
+++ b/solution.py
@@ -11,8 +11,7 @@
 PAD = 1024
 BLOCK = 128
 HALF = 512
-SPLITS = (512, 640)
-SPLITS_SELF = (384, 512)
+SPLITS = ((640, 640), (384, 512), (512, 640))
 SELF_COLS = 768
 F32 = jnp.float32
 BF16 = jnp.bfloat16
@@ -20,7 +19,7 @@
 
 def kernel(
     n_occ, b_in, occ_ref, vir_ref, g_ref,
-    b_ref, vrow, vcol, bp, nbo, nbp, kf, kp, kr, am, ret, rchip, rz,
+    b_ref, vrow, vcol, bp, nbo, nbp, kf, kp, kr, kx, km, am, ret, rchip, rz,
     x_ss, x_rs, z_ss, z_rs, c_ss, c_rs, k_ss, k_rs, a_ss, a_rs, r_ss, r_rs,
 ):
     occ = lax.axis_index("occ")
@@ -111,10 +110,12 @@
         def _():
             chip_send(n, 0)
 
-    def k_cols(k, ab):
-        if k == 0:
-            return pl.ds(HALF, 256) if ab else pl.ds(0, HALF)
-        return ds((o if ab else h) * HALF, HALF)
+    def k_cols(k, ab, part=None):
+        start, size = (HALF if ab else 0, 256 if ab else HALF) if k == 0 else ((o if ab else h) * HALF, HALF)
+        if part is not None:
+            size //= 2
+            start = start + part * size
+        return ds(start, size)
 
     contract = (((1,), (1,)), ((), ()))
 
@@ -135,18 +136,38 @@
             part += lax.dot_general(left_p, bp[right, :], contract, preferred_element_type=F32)
             kf[k, :, cols] = part
             kp[k, :, cols] = part.astype(BF16)
-        for n, (q, dev) in enumerate(((yp, up), (ym, down), (yy, far))):
+        push(kp.at[k, ds(yy * BLOCK, BLOCK), k_cols(k, ab, 0)], relayed(k, ab, 0), k_ss.at[k, ab, 0], k_rs.at[k, ab, 0], up)
+        push(kp.at[k, ds(yy * BLOCK, BLOCK), k_cols(k, ab, 1)], relayed(k, ab, 1), k_ss.at[k, ab, 1], k_rs.at[k, ab, 1], down)
+        push(kp.at[k, ds(yp * BLOCK, BLOCK), k_cols(k, ab, 1)], arrived(k, ab, 0, 1), k_ss.at[k, ab, 2], k_rs.at[k, ab, 2], up)
+        push(kp.at[k, ds(ym * BLOCK, BLOCK), k_cols(k, ab, 0)], arrived(k, ab, 1, 0), k_ss.at[k, ab, 3], k_rs.at[k, ab, 3], down)
+
+    def half_cols(k, ab):
+        return pl.ds(0, 128 if k == 0 and ab else 256)
+
+    def relayed(k, ab, way):
+        return kx.at[k, ab, way, :, half_cols(k, ab)]
+
+    def arrived(k, ab, way, part):
+        return kr.at[k, way, :, k_cols(k, ab, part)]
+
+    def pass_on(k, ab):
+        for way, (source, target, q) in enumerate(((down, up, yp), (up, down, ym))):
+            ref = relayed(k, ab, way)
+            remote(ref, ref, k_rs.at[k, ab, way], k_rs.at[k, ab, way], source).wait_recv()
+            width = half_cols(k, ab)
+            own = kf[k, ds(q * BLOCK, BLOCK), k_cols(k, ab, way)]
+            km[k, ab, way, :, width] = (own + kx[k, ab, way, :, width].astype(F32)).astype(BF16)
             push(
-                kp.at[k, ds(q * BLOCK, BLOCK), cols], kr.at[k, ds(y * BLOCK, BLOCK), cols],
-                k_ss.at[k, ab, n], k_rs.at[k, ab, y], dev,
+                km.at[k, ab, way, :, width], arrived(k, ab, way, way),
+                k_ss.at[k, ab, 4 + way], k_rs.at[k, ab, 4 + way], target,
             )
 
     def amplitude(k):
         for ab in range(2):
             cols = k_cols(k, ab)
-            for q, dev in ((yp, up), (ym, down), (yy, far)):
-                ref = kr.at[k, ds(q * BLOCK, BLOCK), cols]
-                remote(ref, ref, k_rs.at[k, ab, q], k_rs.at[k, ab, q], dev).wait_recv()
+            for n, (way, part) in ((2, (0, 1)), (3, (1, 0)), (4, (0, 0)), (5, (1, 1))):
+                ref = arrived(k, ab, way, part)
+                remote(ref, ref, k_rs.at[k, ab, n], k_rs.at[k, ab, n], up if way else down).wait_recv()
             energy = cols
             if k == 0:
                 energy = ds(o * HALF + lax.rem(y // 2 + h, 2) * 256, 256) if ab else rows_h
@@ -154,15 +175,15 @@
             @pl.loop(0, 4)
             def _(t):
                 total = kf[k, ds(y * BLOCK + t * 32, 32), cols]
-                for q in (yp, ym, yy):
-                    total += kr[k, ds(q * BLOCK + t * 32, 32), cols].astype(F32)
+                for way in range(2):
+                    total += kr[k, way, ds(t * 32, 32), cols].astype(F32)
                 denom = vcol[ds(t * 32, 32), :] + vrow[:, energy] - e_mine - e_pair[k]
                 am[k, ds(base + t * 32, 32), cols] = (total / denom).astype(BF16)
 
     def piece(k, n, side, q, low, w):
         count = 64 if n in (2, 3, 7, 8) else BLOCK
         width = PAD if k else SELF_COLS
-        split = (SPLITS if k else SPLITS_SELF)[w]
+        split = SPLITS[k][w]
         cols = pl.ds(0, width) if n < 5 else pl.ds(0, split) if n < 9 else pl.ds(split, width - split)
         return am.at[k, ds(side * HALF + q * BLOCK + low, count), cols]
 
@@ -277,26 +298,32 @@
             return_part(0, half, rz, z_in).start()
 
     z_send(0)
+    push(b_ref.at[rows_h, :], bp.at[rows_h, :], x_ss.at[1], x_rs.at[1], across)
     own_to_chip(0)
     slot_to_chip(0)
     remote(bp.at[rows_h, :], bp.at[rows_h, :], x_ss.at[0], x_rs.at[0], across).wait_recv()
     z_send(1)
     own_to_chip(1)
-    push(b_ref.at[rows_h, :], bp.at[rows_h, :], x_ss.at[1], x_rs.at[1], across)
     partial_k(0, 0)
     slot_to_chip(1)
     chip_arrive(0)
     chip_arrive(1)
     partial_k(2, 0)
+    pass_on(0, 0)
     partial_k(1, 0)
+    pass_on(2, 0)
     remote(bp.at[rows_o, :], bp.at[rows_o, :], x_ss.at[1], x_rs.at[1], across).wait_recv()
     z_send(2)
     own_to_chip(2)
     partial_k(1, 1)
+    pass_on(1, 0)
     partial_k(2, 1)
+    pass_on(1, 1)
     partial_k(0, 1)
+    pass_on(2, 1)
     amplitude(1)
     stage1(1)
+    pass_on(0, 1)
     slot_to_chip(2)
     amplitude(2)
     stage1(2)
@@ -375,7 +402,9 @@
             pltpu.VMEM((2, HALF, width), BF16),
             pltpu.VMEM((3, HALF, PAD), F32),
             pltpu.VMEM((3, HALF, PAD), BF16),
-            pltpu.VMEM((3, HALF, PAD), BF16),
+            pltpu.VMEM((3, 2, BLOCK, PAD), BF16),
+            pltpu.VMEM((3, 2, 2, BLOCK, 256), BF16),
+            pltpu.VMEM((3, 2, 2, BLOCK, 256), BF16),
             pltpu.VMEM((3, PAD, PAD), BF16),
             pltpu.VMEM((2, PAD, width), BF16),
             pltpu.VMEM((PAD, width), BF16),
@@ -383,7 +412,7 @@
             dma((2,)), dma((2,)),
             dma((3,)), dma((3,)),
             dma((3,)), dma((3,)),
-            dma((3, 2, 3)), dma((3, 2, 4)),
+            dma((3, 2, 6)), dma((3, 2, 6)),
             dma((3, 12)), dma((3, 12)),
             dma((2, 2)), dma((2, 2)),
         ],

time: 119 us -> 112 us (0.941)
  Pallas kernels: 115 us -> 109 us
    pallas_call x1, Pallas kernels: 115 us -> 109 us  [local(): pl.pallas_call(functools.partial(kernel, n_occ), out_shape=jax.ShapeDtype...]
where the time goes in v4:
time: 112 us
  Pallas kernels  109 us (97%)
  local copies, waits for them, and re-layouts  3.04 us (3%)
    pallas_call x1, Pallas kernels, local(): pl.pallas_call(functools.partial(kernel, n_occ), out_shape=jax.ShapeDtype...  109 us
    broadcast_in_dim x1, local copies, waits for them, and re-layouts, local(): return gamma[None, :v]  3.04 us

profile of v4, /device:TPU:2, one launch (start us, length us, event | category | flops | bytes accessed | tf_op | source)
XLA Modules:
  0.0 111.8 jit_solution(13907123129684104523)
XLA Ops:
  0.0 108.7 %shard_map.37 = f32[1024,512]{1,0:T(8,128)} custom-call(bf16[1000,512]{1,0:T(8,128)(2,1)} %bitcast.4, f32[32]{0:T(128)} %occ_ref.1, f32[1,1000]{1,0:T(1,128)} %bitcast.5), custom_call_target="tpu_custom_call" | custom-call | flops 8000000000 | bytes 4000000 | tf_op jit(solution)/shard_map/pallas_call | solution.py:391
  108.7 3.0 %slice_bitcast_fusion = f32[1,1000,512]{2,1,0:T(8,128)} fusion(f32[1024,512]{1,0:T(8,128)} %shard_map.37), kind=kLoop, calls=%fused_computation | loop fusion | bytes 4096000 | tf_op jit(solution)/shard_map/broadcast_in_dim | solution.py:424

commit v5 on v4

--- a/solution.py
+++ b/solution.py
@@ -11,15 +11,16 @@
 PAD = 1024
 BLOCK = 128
 HALF = 512
-SPLITS = ((640, 640), (384, 512), (512, 640))
-SELF_COLS = 768
+SPLITS = ((512, 512), (512, 512), (512, 640))
+SELF_COLS = 640
+SELF_NEAR = 384
 F32 = jnp.float32
 BF16 = jnp.bfloat16
 
 
 def kernel(
     n_occ, b_in, occ_ref, vir_ref, g_ref,
-    b_ref, vrow, vcol, bp, nbo, nbp, kf, kp, kr, kx, km, am, ret, rchip, rz,
+    b_ref, vrow, vwrap, quad, vcol, bp, nbo, nbp, kf, kp, kr, kx, km, am, ret, rchip, rz,
     x_ss, x_rs, z_ss, z_rs, c_ss, c_rs, k_ss, k_rs, a_ss, a_rs, r_ss, r_rs,
 ):
     occ = lax.axis_index("occ")
@@ -56,6 +57,8 @@
     b_ref[whole:, :] = jnp.concatenate([b_in[whole:, :].astype(F32), tail], axis=0).astype(BF16)
     vrow[...] = jnp.ones_like(vrow)
     vrow[:, :v] = vir_ref[...]
+    for n in range(2):
+        vwrap[:, n * HALF:(n + 1) * HALF] = vrow[:, pl.ds(pl.multiple_of(h * HALF, HALF), HALF)]
     base = pl.multiple_of(h * HALF + y * BLOCK, BLOCK)
     here = jnp.broadcast_to(vrow[:, pl.ds(base, BLOCK)], (BLOCK, BLOCK))
     diagonal = lax.broadcasted_iota(jnp.int32, (BLOCK, BLOCK), 0) == lax.broadcasted_iota(jnp.int32, (BLOCK, BLOCK), 1)
@@ -110,12 +113,13 @@
         def _():
             chip_send(n, 0)
 
-    def k_cols(k, ab, part=None):
-        start, size = (HALF if ab else 0, 256 if ab else HALF) if k == 0 else ((o if ab else h) * HALF, HALF)
-        if part is not None:
-            size //= 2
-            start = start + part * size
-        return ds(start, size)
+    def k_cols(k, ab):
+        if k == 0:
+            return pl.ds(SELF_NEAR, 256) if ab else pl.ds(0, SELF_NEAR)
+        return ds((o if ab else h) * HALF, HALF)
+
+    def half_rows(q, part):
+        return ds(q * BLOCK + part * 64, 64)
 
     contract = (((1,), (1,)), ((), ()))
 
@@ -134,28 +138,36 @@
             left, left_p = (b_ref[rows_h, :], bp[rows_h, :]) if k == 0 else (nbo[k - 1, rows_h, :], nbp[k - 1])
             part = lax.dot_general(left, b_ref[right, :], contract, preferred_element_type=F32)
             part += lax.dot_general(left_p, bp[right, :], contract, preferred_element_type=F32)
-            kf[k, :, cols] = part
-            kp[k, :, cols] = part.astype(BF16)
-        push(kp.at[k, ds(yy * BLOCK, BLOCK), k_cols(k, ab, 0)], relayed(k, ab, 0), k_ss.at[k, ab, 0], k_rs.at[k, ab, 0], up)
-        push(kp.at[k, ds(yy * BLOCK, BLOCK), k_cols(k, ab, 1)], relayed(k, ab, 1), k_ss.at[k, ab, 1], k_rs.at[k, ab, 1], down)
-        push(kp.at[k, ds(yp * BLOCK, BLOCK), k_cols(k, ab, 1)], arrived(k, ab, 0, 1), k_ss.at[k, ab, 2], k_rs.at[k, ab, 2], up)
-        push(kp.at[k, ds(ym * BLOCK, BLOCK), k_cols(k, ab, 0)], arrived(k, ab, 1, 0), k_ss.at[k, ab, 3], k_rs.at[k, ab, 3], down)
-
-    def half_cols(k, ab):
-        return pl.ds(0, 128 if k == 0 and ab else 256)
+            if k:
+                kf[k, :, cols] = part
+                kp[k, :, cols] = part.astype(BF16)
+            else:
+                for q in range(4):
+                    for d in range(3):
+                        r, c, at = q * BLOCK, (q + d) % 4 * BLOCK, d * BLOCK
+                        block = part[r:r + BLOCK, c:c + BLOCK]
+                        kf[0, r:r + BLOCK, at:at + BLOCK] = block
+                        kp[0, r:r + BLOCK, at:at + BLOCK] = block.astype(BF16)
+        push(kp.at[k, half_rows(yy, 0), cols], relayed(k, ab, 0), k_ss.at[k, ab, 0], k_rs.at[k, ab, 0], up)
+        push(kp.at[k, half_rows(yy, 1), cols], relayed(k, ab, 1), k_ss.at[k, ab, 1], k_rs.at[k, ab, 1], down)
+        push(kp.at[k, half_rows(yp, 1), cols], arrived(k, ab, 0, 1), k_ss.at[k, ab, 2], k_rs.at[k, ab, 2], up)
+        push(kp.at[k, half_rows(ym, 0), cols], arrived(k, ab, 1, 0), k_ss.at[k, ab, 3], k_rs.at[k, ab, 3], down)
+
+    def run(k, ab):
+        return pl.ds(0, HALF if k else 256 if ab else SELF_NEAR)
 
     def relayed(k, ab, way):
-        return kx.at[k, ab, way, :, half_cols(k, ab)]
+        return kx.at[k, ab, way, :, run(k, ab)]
 
     def arrived(k, ab, way, part):
-        return kr.at[k, way, :, k_cols(k, ab, part)]
+        return kr.at[k, way, pl.ds(part * 64, 64), k_cols(k, ab)]
 
     def pass_on(k, ab):
         for way, (source, target, q) in enumerate(((down, up, yp), (up, down, ym))):
             ref = relayed(k, ab, way)
             remote(ref, ref, k_rs.at[k, ab, way], k_rs.at[k, ab, way], source).wait_recv()
-            width = half_cols(k, ab)
-            own = kf[k, ds(q * BLOCK, BLOCK), k_cols(k, ab, way)]
+            width = run(k, ab)
+            own = kf[k, half_rows(q, way), k_cols(k, ab)]
             km[k, ab, way, :, width] = (own + kx[k, ab, way, :, width].astype(F32)).astype(BF16)
             push(
                 km.at[k, ab, way, :, width], arrived(k, ab, way, way),
@@ -168,16 +180,18 @@
             for n, (way, part) in ((2, (0, 1)), (3, (1, 0)), (4, (0, 0)), (5, (1, 1))):
                 ref = arrived(k, ab, way, part)
                 remote(ref, ref, k_rs.at[k, ab, n], k_rs.at[k, ab, n], up if way else down).wait_recv()
-            energy = cols
-            if k == 0:
-                energy = ds(o * HALF + lax.rem(y // 2 + h, 2) * 256, 256) if ab else rows_h
+            source, energy = vrow, cols
+            if k == 0 and ab:
+                energy = ds(o * HALF + lax.rem(y // 2 + h, 2) * 256, 256)
+            elif k == 0:
+                source, energy = vwrap, pl.ds(pl.multiple_of(y * BLOCK, BLOCK), SELF_NEAR)
 
             @pl.loop(0, 4)
             def _(t):
                 total = kf[k, ds(y * BLOCK + t * 32, 32), cols]
                 for way in range(2):
                     total += kr[k, way, ds(t * 32, 32), cols].astype(F32)
-                denom = vcol[ds(t * 32, 32), :] + vrow[:, energy] - e_mine - e_pair[k]
+                denom = vcol[ds(t * 32, 32), :] + source[:, energy] - e_mine - e_pair[k]
                 am[k, ds(base + t * 32, 32), cols] = (total / denom).astype(BF16)
 
     def piece(k, n, side, q, low, w):
@@ -260,13 +274,19 @@
 
     def self_product():
         for side in range(2):
+            for q in range(4):
+                r, last = q * BLOCK, (q + 3) % 4 * BLOCK
+                for d in range(3):
+                    c = (q + d) % 4 * BLOCK
+                    quad[r:r + BLOCK, c:c + BLOCK] = am[0, pl.ds(side * HALF + r, BLOCK), pl.ds(d * BLOCK, BLOCK)]
+                quad[r:r + BLOCK, last:last + BLOCK] = am[0, pl.ds(side * HALF + last, BLOCK), pl.ds(BLOCK, BLOCK)].T
             r = pl.ds(side * HALF, HALF)
-            g_ref[r, :] += jnp.dot(am[0, r, pl.ds(0, HALF)], b_ref[r, :], preferred_element_type=F32)
+            g_ref[r, :] += jnp.dot(quad[...], b_ref[r, :], preferred_element_type=F32)
         for side in range(2):
             for s in range(2):
                 r = pl.ds(side * HALF + s * 256, 256)
                 c = pl.ds((1 - side) * HALF + (s + side) % 2 * 256, 256)
-                block = am[0, r, pl.ds(HALF, 256)]
+                block = am[0, r, pl.ds(SELF_NEAR, 256)]
                 g_ref[r, :] += jnp.dot(block, b_ref[c, :], preferred_element_type=F32)
                 g_ref[c, :] += lax.dot_general(block, b_ref[r, :], (((0,), (0,)), ((), ())), preferred_element_type=F32)
 
@@ -396,6 +416,8 @@
         scratch_shapes=[
             pltpu.VMEM((PAD, width), BF16),
             pltpu.VMEM((1, PAD), F32),
+            pltpu.VMEM((1, PAD), F32),
+            pltpu.VMEM((HALF, HALF), BF16),
             pltpu.VMEM((BLOCK, 1), F32),
             pltpu.VMEM((PAD, width), BF16),
             pltpu.VMEM((2, PAD, width), BF16),
@@ -403,8 +425,8 @@
             pltpu.VMEM((3, HALF, PAD), F32),
             pltpu.VMEM((3, HALF, PAD), BF16),
             pltpu.VMEM((3, 2, BLOCK, PAD), BF16),
-            pltpu.VMEM((3, 2, 2, BLOCK, 256), BF16),
-            pltpu.VMEM((3, 2, 2, BLOCK, 256), BF16),
+            pltpu.VMEM((3, 2, 2, 64, HALF), BF16),
+            pltpu.VMEM((3, 2, 2, 64, HALF), BF16),
             pltpu.VMEM((3, PAD, PAD), BF16),
             pltpu.VMEM((2, PAD, width), BF16),
             pltpu.VMEM((PAD, width), BF16),

time: 112 us -> 111 us (level)
    pallas_call x1, Pallas kernels: 109 us -> 108 us  [local(): pl.pallas_call(functools.partial(kernel, n_occ), out_shape=jax.ShapeDtype...]
where the time goes in v5:
time: 111 us
  Pallas kernels  108 us (97%)
  local copies, waits for them, and re-layouts  3.04 us (3%)
    pallas_call x1, Pallas kernels, local(): pl.pallas_call(functools.partial(kernel, n_occ), out_shape=jax.ShapeDtype...  108 us
    broadcast_in_dim x1, local copies, waits for them, and re-layouts, local(): return gamma[None, :v]  3.04 us

profile of v5, /device:TPU:2, one launch (start us, length us, event | category | flops | bytes accessed | tf_op | source)
XLA Modules:
  0.0 110.6 jit_solution(1777764391301962151)
XLA Ops:
  0.0 107.6 %shard_map.37 = f32[1024,512]{1,0:T(8,128)} custom-call(bf16[1000,512]{1,0:T(8,128)(2,1)} %bitcast.4, f32[32]{0:T(128)} %occ_ref.1, f32[1,1000]{1,0:T(1,128)} %bitcast.5), custom_call_target="tpu_custom_call" | custom-call | flops 8000000000 | bytes 4000000 | tf_op jit(solution)/shard_map/pallas_call | solution.py:411
  107.6 3.0 %slice_bitcast_fusion = f32[1,1000,512]{2,1,0:T(8,128)} fusion(f32[1024,512]{1,0:T(8,128)} %shard_map.37), kind=kLoop, calls=%fused_computation | loop fusion | bytes 4096000 | tf_op jit(solution)/shard_map/broadcast_in_dim | solution.py:446

commit v6 on v5

--- a/solution.py
+++ b/solution.py
@@ -272,23 +272,21 @@
 
         return store
 
-    def self_product():
-        for side in range(2):
-            for q in range(4):
-                r, last = q * BLOCK, (q + 3) % 4 * BLOCK
-                for d in range(3):
-                    c = (q + d) % 4 * BLOCK
-                    quad[r:r + BLOCK, c:c + BLOCK] = am[0, pl.ds(side * HALF + r, BLOCK), pl.ds(d * BLOCK, BLOCK)]
-                quad[r:r + BLOCK, last:last + BLOCK] = am[0, pl.ds(side * HALF + last, BLOCK), pl.ds(BLOCK, BLOCK)].T
-            r = pl.ds(side * HALF, HALF)
-            g_ref[r, :] += jnp.dot(quad[...], b_ref[r, :], preferred_element_type=F32)
-        for side in range(2):
-            for s in range(2):
-                r = pl.ds(side * HALF + s * 256, 256)
-                c = pl.ds((1 - side) * HALF + (s + side) % 2 * 256, 256)
-                block = am[0, r, pl.ds(SELF_NEAR, 256)]
-                g_ref[r, :] += jnp.dot(block, b_ref[c, :], preferred_element_type=F32)
-                g_ref[c, :] += lax.dot_general(block, b_ref[r, :], (((0,), (0,)), ((), ())), preferred_element_type=F32)
+    def self_product(side):
+        for q in range(4):
+            r, last = q * BLOCK, (q + 3) % 4 * BLOCK
+            for d in range(3):
+                c = (q + d) % 4 * BLOCK
+                quad[r:r + BLOCK, c:c + BLOCK] = am[0, ds(side * HALF + r, BLOCK), pl.ds(d * BLOCK, BLOCK)]
+            quad[r:r + BLOCK, last:last + BLOCK] = am[0, ds(side * HALF + last, BLOCK), pl.ds(BLOCK, BLOCK)].T
+        r = ds(side * HALF, HALF)
+        g_ref[r, :] += jnp.dot(quad[...], b_ref[r, :], preferred_element_type=F32)
+        for s in range(2):
+            r = ds(side * HALF + s * 256, 256)
+            c = ds((1 - side) * HALF + lax.rem(s + side, 2) * 256, 256)
+            block = am[0, r, pl.ds(SELF_NEAR, 256)]
+            g_ref[r, :] += jnp.dot(block, b_ref[c, :], preferred_element_type=F32)
+            g_ref[c, :] += lax.dot_general(block, b_ref[r, :], (((0,), (0,)), ((), ())), preferred_element_type=F32)
 
     def return_part(n, half, dst, dev):
         rows = rows_o if half else rows_h
@@ -366,8 +364,9 @@
     stage4(2)
     give_back(2, 1)
     product(2, True, nbo[1], add_gamma)
+    self_product(h)
     stage4(0)
-    self_product()
+    self_product(o)
     for half in range(2):
         return_part(1, half, rz, z_out).wait_recv()
 

time: 111 us -> 111 us (level)
  no operation moved by 1% of the time
where the time goes in v6:
time: 111 us
  Pallas kernels  108 us (97%)
  local copies, waits for them, and re-layouts  3.04 us (3%)
    pallas_call x1, Pallas kernels, local(): pl.pallas_call(functools.partial(kernel, n_occ), out_shape=jax.ShapeDtype...  108 us
    broadcast_in_dim x1, local copies, waits for them, and re-layouts, local(): return gamma[None, :v]  3.04 us

profile of v6, /device:TPU:2, one launch (start us, length us, event | category | flops | bytes accessed | tf_op | source)
XLA Modules:
  0.0 110.6 jit_solution(4912410739868752197)
XLA Ops:
  0.0 107.6 %shard_map.37 = f32[1024,512]{1,0:T(8,128)} custom-call(bf16[1000,512]{1,0:T(8,128)(2,1)} %bitcast.4, f32[32]{0:T(128)} %occ_ref.1, f32[1,1000]{1,0:T(1,128)} %bitcast.5), custom_call_target="tpu_custom_call" | custom-call | flops 8000000000 | bytes 4000000 | tf_op jit(solution)/shard_map/pallas_call | solution.py:410
  107.6 3.0 %slice_bitcast_fusion = f32[1,1000,512]{2,1,0:T(8,128)} fusion(f32[1024,512]{1,0:T(8,128)} %shard_map.37), kind=kLoop, calls=%fused_computation | loop fusion | bytes 4096000 | tf_op jit(solution)/shard_map/broadcast_in_dim | solution.py:445
